TPU v7x, 32 devices: a whole 2x2x4 slice. The times are simulated.
32 devices in a mesh: blk: 8 (over z, x), win: 4 (over y, core).
Axes of the slice: x: 2, y: 2, z: 4, core: 2. Of those that a mesh axis runs over, the one named last changes fastest.
Arguments:
- samples: bfloat16 [1024, 32, 2048], P('blk', 'win'), may hold values from -6 to 6
- pair_offsets: int32 [24], P('blk'), may hold values from 0 to 4, as said below
- pair_count: int32 [8], P('blk'), may hold values from 1 to 3
Outputs:
- cross_spectra: bfloat16 [24, 128, 2, 128, 128], P('blk', 'win')
Inputs may be any that keep to these rules, and one draw needn't show every extreme that they name: `pair_offsets`: entry w * 3 + s belongs to worker w. The live slots of a worker (s below its count) hold different offsets, with w + offset below the number of blocks; the other slots hold 0.
All inputs are finite; a program needn't handle non-finite values.
Results may differ from a plain program's by a relative error of at most 0.0068.
Values may be sent and summed in bfloat16 or wider, within the bound.
A program may use at most 64 MiB of HBM per device.

v0:
```python
import math
import jax
import jax.numpy as jnp
from jax import lax
from jax.sharding import PartitionSpec as P

BINS = 128
BIN0 = 32
SMOOTH = 4
OFFSET = 4
water_level = 0.1
epsilon = 1e-06


def shifted(block, axis, distance):
    devices = range(lax.axis_size(axis))
    route = [(i - distance, i) for i in devices if i - distance in devices]
    return lax.ppermute(block, axis, route)


def dft_table(length):
    sample_idx = jnp.arange(length, dtype=jnp.int32)
    bin_freqs = BIN0 + jnp.arange(BINS, dtype=jnp.int32)
    phases = sample_idx[:, None] * bin_freqs[None, :] % length
    angles = phases.astype(jnp.float32) * (2.0 * math.pi / length)
    window_taper = 0.5 - 0.5 * jnp.cos(
        (sample_idx.astype(jnp.float32) + 0.5) * (2.0 * math.pi / length)
    )
    cosines = window_taper[:, None] * jnp.cos(angles)
    sines = -window_taper[:, None] * jnp.sin(angles)
    return jnp.concatenate([cosines, sines], axis=1).astype(jnp.bfloat16)


def band_weights():
    bin_index = jnp.arange(BINS, dtype=jnp.int32)
    inside = (jnp.abs(bin_index[:, None] - bin_index[None, :]) <= SMOOTH).astype(jnp.float32)
    return inside / jnp.sum(inside, axis=0, keepdims=True)


def whiten_spectrum(spectrum, weights):
    energy = spectrum[:, 0] * spectrum[:, 0] + spectrum[:, 1] * spectrum[:, 1]
    smoothed = jnp.einsum("wjc,jb->wbc", energy, weights, precision=lax.Precision.HIGHEST)
    average = jnp.mean(energy, axis=1, keepdims=True)
    factor = lax.rsqrt(smoothed + water_level * average + epsilon)
    return (spectrum * factor[:, None]).astype(jnp.bfloat16)


def cross_pair(left_side, partner, windows):
    right_side = partner.reshape(2 * windows, partner.shape[2], partner.shape[3])
    product = lax.dot_general(
        left_side, right_side, (((1,), (0,)), ((2,), (1,))), preferred_element_type=jnp.float32
    )
    return product * (1.0 / windows)


def shards(samples, pair_offsets, pair_count):
    channels, win_dev, length = samples.shape
    table = dft_table(length)
    weights = band_weights()
    spectrum = jnp.einsum("cwt,tk->wkc", samples, table, preferred_element_type=jnp.float32)
    whitened = whiten_spectrum(spectrum.reshape(win_dev, 2, BINS, channels), weights)
    by_bins = lax.all_to_all(whitened, "win", split_axis=2, concat_axis=0, tiled=True)
    windows = by_bins.shape[0]
    bins_dev = by_bins.shape[2]
    swapped = jnp.stack([by_bins[:, 1], -by_bins[:, 0]], axis=1)
    left_side = jnp.stack([by_bins, swapped], axis=0).reshape(2, 2 * windows, bins_dev, channels)
    neighbours = [by_bins]
    for distance in range(1, OFFSET + 1):
        neighbours.append(shifted(by_bins, "blk", -distance))
    nearby = jnp.stack(neighbours, axis=0)
    live_count = pair_count[0]
    slot_total = pair_offsets.shape[0]
    results = []
    for slot_rank in range(slot_total):
        partner = lax.dynamic_index_in_dim(nearby, pair_offsets[slot_rank], 0, keepdims=False)
        value = cross_pair(left_side, partner, windows)
        results.append(
            jnp.where(slot_rank < live_count, value, jnp.zeros_like(value)).astype(jnp.bfloat16)
        )
    cross_spectra = jnp.stack(results, axis=0)
    return cross_spectra


def solution(mesh):
    in_specs = (P("blk", "win", None), P("blk"), P("blk"))
    out_specs = P("blk", "win", None, None, None)
    return jax.shard_map(shards, mesh=mesh, in_specs=in_specs, out_specs=out_specs, check_vma=False)
```

profile of v0, /device:TPU:0, one launch (start us, length us, event | category | flops | bytes accessed | tf_op | source)
XLA Modules:
  0.0 109.8 jit_solution(9315533526000073080)
XLA Ops:
  0.0 0.1 convert_reduce_fusion
  0.1 0.1 multiply_subtract_fusion
  0.2 4.5 %multiply_convert_fusion.2 = (bf16[2048,128]{0,1:T(8,128)(2,1)S(1)}, bf16[2048,128]{0,1:T(8,128)(2,1)S(1)}) fusion(s32[128]{0:T(128)S(1)} %iota_add_fusion, f32[2048]{0:T(1024)S(1)} %get-tuple-element.15, f32[2048]{0:T(1024)S(1)} %get-tuple-element.16), kind=kLoop, calls=%fused_computation.25 | loop fusion | flops 4718592 | bytes 1065472 | tf_op jit(solution)/shard_map/convert
  4.7 7.1 %fusion = f32[256,128,8]{1,0,2:T(8,128)S(1)} fusion(bf16[128,8,2048]{2,1,0:T(8,128)(2,1)} %param.3, bf16[2048,128]{0,1:T(8,128)(2,1)S(1)} %get-tuple-element.14, bf16[2048,128]{0,1:T(8,128)(2,1)S(1)} %get-tuple-element.13), kind=kOutput, calls=%fused_computation.1 | convolution fusion | flops 1075838976 | bytes 6291456 | tf_op jit(solution)/shard_map/cwt,tk->wkc/dot_general | solution.py:60
  11.9 0.1 fusion.18
  12.0 0.0 copy-start
  12.0 0.6 fusion.7
  12.7 0.1 multiply_convert_fusion
  12.8 1.3 %copy.15 = bf16[8,2,128,128]{3,1,0,2:T(2,128)(2,1)} copy(bf16[8,2,128,128]{3,2,1,0:T(8,128)(2,1)S(1)} %multiply_convert_fusion) | data formatting | bytes 1048576 | tf_op jit(solution)/shard_map/convert_element_type | solution.py:45
  14.1 4.2 %all-to-all-start = ((bf16[8,2,128,128]{3,1,0,2:T(2,128)(2,1)}), bf16[8,2,128,128]{3,1,0,2:T(2,128)(2,1)S(1)}, u32[]{:S(2)}, u32[]{:S(2)}) async-start(bf16[8,2,128,128]{3,1,0,2:T(2,128)(2,1)} %copy.15), calls=%async_computation | async-start | bytes 1048576 | tf_op jit(solution)/shard_map/all_to_all | solution.py:62
  18.3 0.7 fusion.31
  25.2 1.9 %all-to-all-done = bf16[8,2,128,128]{3,1,0,2:T(2,128)(2,1)S(1)} async-done(((bf16[8,2,128,128]{3,1,0,2:T(2,128)(2,1)}), bf16[8,2,128,128]{3,1,0,2:T(2,128)(2,1)S(1)}, u32[]{:S(2)}, u32[]{:S(2)}) %all-to-all-start) | async-done | bytes 524320 | tf_op jit(solution)/shard_map/all_to_all | solution.py:62
  27.2 0.5 copy.16
  27.7 1.3 %collective-permute-start.2 = (bf16[32,2,32,128]{3,1,0,2:T(2,128)(2,1)S(1)}, bf16[32,2,32,128]{3,1,0,2:T(2,128)(2,1)S(1)}, u32[]{:S(2)}, u32[]{:S(2)}) collective-permute-start(bf16[32,2,32,128]{3,1,0,2:T(2,128)(2,1)S(1)} %bitcast.62), channel_id=1, source_target_pairs={{12,0},{16,4},{20,8},{24,12},{28,16},{13,1},{17,5},{21,9},{25,13},... | collective-permute-start | bytes 1572872 | tf_op jit(solution)/shard_map/ppermute | solution.py:18
  29.0 1.3 %collective-permute-start.1 = (bf16[32,2,32,128]{3,1,0,2:T(2,128)(2,1)S(1)}, bf16[32,2,32,128]{3,1,0,2:T(2,128)(2,1)S(1)}, u32[]{:S(2)}, u32[]{:S(2)}) collective-permute-start(bf16[32,2,32,128]{3,1,0,2:T(2,128)(2,1)S(1)} %bitcast.63), channel_id=1, source_target_pairs={{8,0},{12,4},{16,8},{20,12},{24,16},{28,20},{9,1},{13,5},{17,9},{2... | collective-permute-start | bytes 1572872 | tf_op jit(solution)/shard_map/ppermute | solution.py:18
  30.3 1.3 %collective-permute-start = (bf16[32,2,32,128]{3,1,0,2:T(2,128)(2,1)S(1)}, bf16[32,2,32,128]{3,1,0,2:T(2,128)(2,1)S(1)}, u32[]{:S(2)}, u32[]{:S(2)}) collective-permute-start(bf16[32,2,32,128]{3,1,0,2:T(2,128)(2,1)S(1)} %bitcast.64), channel_id=1, source_target_pairs={{4,0},{8,4},{12,8},{16,12},{20,16},{24,20},{28,24},{5,1},{9,5},{13... | collective-permute-start | bytes 1572872 | tf_op jit(solution)/shard_map/ppermute | solution.py:18
  31.6 1.5 %collective-permute-start.3 = (bf16[32,2,32,128]{3,1,0,2:T(2,128)(2,1)S(1)}, bf16[32,2,32,128]{3,1,0,2:T(2,128)(2,1)S(1)}, u32[]{:S(2)}, u32[]{:S(2)}) collective-permute-start(bf16[32,2,32,128]{3,1,0,2:T(2,128)(2,1)S(1)} %bitcast.65), channel_id=1, source_target_pairs={{16,0},{20,4},{24,8},{28,12},{17,1},{21,5},{25,9},{29,13},{18,2},{... | collective-permute-start | bytes 1572872 | tf_op jit(solution)/shard_map/ppermute | solution.py:18
  33.1 0.9 fusion.30
  34.1 0.4 constant_dynamic-update-slice_fusion
  34.5 1.2 %pad_maximum_fusion.2 = bf16[32,2,32,128]{3,1,0,2:T(2,128)(2,1)S(1)} fusion(bf16[32,1,32,128]{3,1,0,2:T(2,128)(2,1)S(1)} %get-tuple-element.9, bf16[32,1,32,128]{3,1,0,2:T(2,128)(2,1)S(1)} %get-tuple-element.8), kind=kLoop, calls=%fused_computation.33 | loop fusion | flops 1048576 | bytes 1048576 | tf_op jit(solution)/shard_map/stack | solution.py:65
  35.7 20.0 %collective-permute-done = bf16[32,2,32,128]{3,1,0,2:T(2,128)(2,1)S(1)} collective-permute-done((bf16[32,2,32,128]{3,1,0,2:T(2,128)(2,1)S(1)}, bf16[32,2,32,128]{3,1,0,2:T(2,128)(2,1)S(1)}, u32[]{:S(2)}, u32[]{:S(2)}) %collective-permute-start) | collective-permute-done | bytes 524320 | tf_op jit(solution)/shard_map/ppermute | solution.py:18
  55.7 0.5 bitcast_dynamic-update-slice_fusion.3
  56.2 0.0 collective-permute-done.1
  56.3 0.5 bitcast_dynamic-update-slice_fusion.2
  56.8 0.5 bitcast_dynamic-update-slice_fusion.1
  57.3 44.6 %collective-permute-done.3 = bf16[32,2,32,128]{3,1,0,2:T(2,128)(2,1)S(1)} collective-permute-done((bf16[32,2,32,128]{3,1,0,2:T(2,128)(2,1)S(1)}, bf16[32,2,32,128]{3,1,0,2:T(2,128)(2,1)S(1)}, u32[]{:S(2)}, u32[]{:S(2)}) %collective-permute-start.3) | collective-permute-done | bytes 524320 | tf_op jit(solution)/shard_map/ppermute | solution.py:18
  101.8 0.5 bitcast_dynamic-update-slice_fusion
  102.3 1.5 %constant_dynamic-slice_fusion.2 = (bf16[1,32,2,32,128]{4,2,1,3,0:T(2,128)(2,1)S(1)}, bf16[1,32,2,32,128]{4,2,1,3,0:T(2,128)(2,1)S(1)}, bf16[1,32,2,32,128]{4,2,1,3,0:T(2,128)(2,1)S(1)}) fusion(bf16[5,32,2,32,128]{4,2,1,3,0:T(2,128)(2,1)S(1)} %bitcast_dynamic-update-slice_fusion, s32[]{:T(128)S(6)} %select_n.41, s32[]{:T(128)S(6)} %select_n.47, s32[]{:T(128)S(6)} %select_n.44), kind=kLoop, calls=%fused_computation.52 | loop fusion | bytes 3145740 | tf_op jit(solution)/shard_map/jit(dynamic_index_in_dim)/dynamic_slice | solution.py:75
  103.8 0.9 fusion.4
  104.7 0.9 fusion.2
  105.7 0.9 fusion.3
  106.6 3.2 %pad_maximum_fusion = bf16[3,32,2,128,128]{4,3,2,1,0:T(8,128)(2,1)} fusion(bf16[1,32,2,128,128]{4,3,2,1,0:T(8,128)(2,1)S(1)} %fusion.4, bf16[1,32,2,128,128]{4,3,2,1,0:T(8,128)(2,1)S(1)} %fusion.3, bf16[1,32,2,128,128]{4,3,2,1,0:T(8,128)(2,1)S(1)} %fusion.2), kind=kLoop, calls=%fused_computation | loop fusion | flops 6291456 | bytes 12582912 | tf_op jit(solution)/shard_map/stack | solution.py:80
  (4 shorter events, 0.0 us)
Async XLA Ops:
  12.0 6.4 %copy-start = (s32[3]{0:T(128)S(1)}, s32[3]{0:T(128)}, u32[]{:S(2)}) copy-start(s32[3]{0:T(128)} %param.4) | copy-start | bytes 40
  14.1 13.1 %all-to-all-start = ((bf16[8,2,128,128]{3,1,0,2:T(2,128)(2,1)}), bf16[8,2,128,128]{3,1,0,2:T(2,128)(2,1)S(1)}, u32[]{:S(2)}, u32[]{:S(2)}) async-start(bf16[8,2,128,128]{3,1,0,2:T(2,128)(2,1)} %copy.15), calls=%async_computation | async-start | bytes 1048576 | tf_op jit(solution)/shard_map/all_to_all | solution.py:62
  27.7 29.0 %collective-permute-start.2 = (bf16[32,2,32,128]{3,1,0,2:T(2,128)(2,1)S(1)}, bf16[32,2,32,128]{3,1,0,2:T(2,128)(2,1)S(1)}, u32[]{:S(2)}, u32[]{:S(2)}) collective-permute-start(bf16[32,2,32,128]{3,1,0,2:T(2,128)(2,1)S(1)} %bitcast.62), channel_id=1, source_target_pairs={{12,0},{16,4},{20,8},{24,12},{28,16},{13,1},{17,5},{21,9},{25,13},... | collective-permute-start | bytes 1572872 | tf_op jit(solution)/shard_map/ppermute | solution.py:18
  29.0 27.2 %collective-permute-start.1 = (bf16[32,2,32,128]{3,1,0,2:T(2,128)(2,1)S(1)}, bf16[32,2,32,128]{3,1,0,2:T(2,128)(2,1)S(1)}, u32[]{:S(2)}, u32[]{:S(2)}) collective-permute-start(bf16[32,2,32,128]{3,1,0,2:T(2,128)(2,1)S(1)} %bitcast.63), channel_id=1, source_target_pairs={{8,0},{12,4},{16,8},{20,12},{24,16},{28,20},{9,1},{13,5},{17,9},{2... | collective-permute-start | bytes 1572872 | tf_op jit(solution)/shard_map/ppermute | solution.py:18
  30.3 25.4 %collective-permute-start = (bf16[32,2,32,128]{3,1,0,2:T(2,128)(2,1)S(1)}, bf16[32,2,32,128]{3,1,0,2:T(2,128)(2,1)S(1)}, u32[]{:S(2)}, u32[]{:S(2)}) collective-permute-start(bf16[32,2,32,128]{3,1,0,2:T(2,128)(2,1)S(1)} %bitcast.64), channel_id=1, source_target_pairs={{4,0},{8,4},{12,8},{16,12},{20,16},{24,20},{28,24},{5,1},{9,5},{13... | collective-permute-start | bytes 1572872 | tf_op jit(solution)/shard_map/ppermute | solution.py:18
  31.6 70.2 %collective-permute-start.3 = (bf16[32,2,32,128]{3,1,0,2:T(2,128)(2,1)S(1)}, bf16[32,2,32,128]{3,1,0,2:T(2,128)(2,1)S(1)}, u32[]{:S(2)}, u32[]{:S(2)}) collective-permute-start(bf16[32,2,32,128]{3,1,0,2:T(2,128)(2,1)S(1)} %bitcast.65), channel_id=1, source_target_pairs={{16,0},{20,4},{24,8},{28,12},{17,1},{21,5},{25,9},{29,13},{18,2},{... | collective-permute-start | bytes 1572872 | tf_op jit(solution)/shard_map/ppermute | solution.py:18
where the time goes:
time: 110 us
  waiting for transfers between devices  66.6 us (61%)
  matrix products  10.6 us (10%)
  other arithmetic  10.2 us (9%)
  starting transfers between devices  9.58 us (9%)
  between operations  6.46 us (6%)
  local copies, waits for them, and re-layouts  6.39 us (6%)
    ppermute x4, waiting for transfers between devices, shifted(): return lax.ppermute(block, axis, route)  64.6 us
    dot_general x1, matrix products, shards(): jnp.einsum('cwt,tk->wkc', samples, table, preferred_element_type=jnp.floa...  7.15 us
    ppermute x4, starting transfers between devices, shifted(): return lax.ppermute(block, axis, route)  5.35 us
    another operation x1, other arithmetic  4.53 us
    all_to_all x1, starting transfers between devices, shards(): lax.all_to_all(whitened, 'win', split_axis=2, concat_axis=0, tiled=True)  4.24 us
    another operation x1, other arithmetic, shards(): cross_spectra = jnp.stack(results, axis=0)  3.15 us
    dot_general x3, matrix products, cross_pair(): lax.dot_general(left_side, right_side, (((1,), (0,)), ((2,), (1,))), pref...  2.8 us
  transfers between devices with their start and end apart: 5, of which 3 were waited for; matrix products, arithmetic and copies ran while one was open for 4% of the time, Pallas kernels for 0%

commit v1 on v0

--- a/solution.py
+++ b/solution.py
@@ -10,6 +10,12 @@
 OFFSET = 4
 water_level = 0.1
 epsilon = 1e-06
+
+
+def swap_blocks(array, axis, split, join):
+    pieces = jnp.split(array, lax.axis_size(axis), axis=split)
+    arrived = lax.all_to_all(jnp.stack(pieces), axis, 0, 0)
+    return jnp.concatenate(arrived, axis=join)
 
 
 def shifted(block, axis, distance):
@@ -59,7 +65,7 @@
     weights = band_weights()
     spectrum = jnp.einsum("cwt,tk->wkc", samples, table, preferred_element_type=jnp.float32)
     whitened = whiten_spectrum(spectrum.reshape(win_dev, 2, BINS, channels), weights)
-    by_bins = lax.all_to_all(whitened, "win", split_axis=2, concat_axis=0, tiled=True)
+    by_bins = swap_blocks(whitened, "win", 2, 0)
     windows = by_bins.shape[0]
     bins_dev = by_bins.shape[2]
     swapped = jnp.stack([by_bins[:, 1], -by_bins[:, 0]], axis=1)

time: 110 us -> 110 us (level)
    convert_element_type x1 -> x0, local copies, waits for them, and re-layouts: 1.33 us -> none  [whiten_spectrum(): return (spectrum * factor[:, None]).astype(jnp.bfloat16)]
    another operation x1 -> x2, other arithmetic: 4.53 us -> 5.4 us
  transfers between devices with their start and end apart: 5 -> 5, of which waited for: 3 -> 3; matrix products, arithmetic and copies ran while one was open for 4% -> 5% of each run, Pallas kernels for 0% -> 0%
where the time goes in v1:
time: 110 us; the launch traced here: 109 us
  waiting for transfers between devices  65.7 us (60%)
  other arithmetic  11.1 us (10%)
  matrix products  10.6 us (10%)
  starting transfers between devices  9.58 us (9%)
  between operations  6.7 us (6%)
  local copies, waits for them, and re-layouts  5.76 us (5%)
    ppermute x4, waiting for transfers between devices, shifted(): return lax.ppermute(block, axis, route)  63.9 us
    dot_general x1, matrix products, shards(): jnp.einsum('cwt,tk->wkc', samples, table, preferred_element_type=jnp.floa...  7.15 us
    ppermute x4, starting transfers between devices, shifted(): return lax.ppermute(block, axis, route)  5.35 us
    another operation x1, other arithmetic  4.53 us
    all_to_all x1, starting transfers between devices, swap_blocks(): arrived = lax.all_to_all(jnp.stack(pieces), axis, 0, 0)  4.24 us
    another operation x1, other arithmetic, shards(): cross_spectra = jnp.stack(results, axis=0)  3.15 us
    dot_general x3, matrix products, cross_pair(): lax.dot_general(left_side, right_side, (((1,), (0,)), ((2,), (1,))), pref...  2.82 us
  transfers between devices with their start and end apart: 5, of which 3 were waited for; matrix products, arithmetic and copies ran while one was open for 5% of the time, Pallas kernels for 0%

profile of v1, /device:TPU:0, one launch (start us, length us, event | category | flops | bytes accessed | tf_op | source)
XLA Modules:
  0.0 109.4 jit_solution(18362155260087869472)
XLA Ops:
  0.0 0.1 convert_reduce_fusion
  0.1 0.1 multiply_subtract_fusion
  0.2 4.5 %multiply_convert_fusion.2 = (bf16[2048,128]{0,1:T(8,128)(2,1)S(1)}, bf16[2048,128]{0,1:T(8,128)(2,1)S(1)}) fusion(s32[128]{0:T(128)S(1)} %iota_add_fusion, f32[2048]{0:T(1024)S(1)} %get-tuple-element.19, f32[2048]{0:T(1024)S(1)} %get-tuple-element.20), kind=kLoop, calls=%fused_computation.25 | loop fusion | flops 4718592 | bytes 1065472 | tf_op jit(solution)/shard_map/convert
  4.7 7.1 %fusion = f32[256,128,8]{1,0,2:T(8,128)S(1)} fusion(bf16[128,8,2048]{2,1,0:T(8,128)(2,1)} %param.3, bf16[2048,128]{0,1:T(8,128)(2,1)S(1)} %get-tuple-element.18, bf16[2048,128]{0,1:T(8,128)(2,1)S(1)} %get-tuple-element.17), kind=kOutput, calls=%fused_computation.1 | convolution fusion | flops 1075838976 | bytes 6291456 | tf_op jit(solution)/shard_map/cwt,tk->wkc/dot_general | solution.py:66
  11.9 0.1 fusion.20
  12.0 0.6 fusion.7
  12.6 0.1 multiply_convert_fusion
  12.8 0.1 slice_bitcast_fusion.5
  12.8 0.9 pad_maximum_fusion.2
  13.7 4.2 %all-to-all-start = ((bf16[4,8,2,32,128]{4,3,2,1,0:T(8,128)(2,1)}), bf16[4,8,2,32,128]{4,3,2,1,0:T(8,128)(2,1)S(1)}, u32[]{:S(2)}, u32[]{:S(2)}) async-start(bf16[4,8,2,32,128]{4,3,2,1,0:T(8,128)(2,1)} %pad_maximum_fusion.2), calls=%async_computation | async-start | bytes 1048576 | tf_op jit(solution)/shard_map/all_to_all | solution.py:17
  17.9 0.6 fusion.33
  25.0 1.7 %all-to-all-done = bf16[4,8,2,32,128]{4,3,2,1,0:T(8,128)(2,1)S(1)} async-done(((bf16[4,8,2,32,128]{4,3,2,1,0:T(8,128)(2,1)}), bf16[4,8,2,32,128]{4,3,2,1,0:T(8,128)(2,1)S(1)}, u32[]{:S(2)}, u32[]{:S(2)}) %all-to-all-start) | async-done | bytes 524320 | tf_op jit(solution)/shard_map/all_to_all | solution.py:17
  26.8 0.5 copy.8
  27.3 1.3 %collective-permute-start.2 = (bf16[32,2,32,128]{3,1,0,2:T(2,128)(2,1)S(1)}, bf16[32,2,32,128]{3,1,0,2:T(2,128)(2,1)S(1)}, u32[]{:S(2)}, u32[]{:S(2)}) collective-permute-start(bf16[32,2,32,128]{3,1,0,2:T(2,128)(2,1)S(1)} %copy.8), channel_id=1, source_target_pairs={{12,0},{16,4},{20,8},{24,12},{28,16},{13,1},{17,5},{21,9},{25,13},... | collective-permute-start | bytes 1572872 | tf_op jit(solution)/shard_map/ppermute | solution.py:24
  28.6 1.3 %collective-permute-start.1 = (bf16[32,2,32,128]{3,1,0,2:T(2,128)(2,1)S(1)}, bf16[32,2,32,128]{3,1,0,2:T(2,128)(2,1)S(1)}, u32[]{:S(2)}, u32[]{:S(2)}) collective-permute-start(bf16[32,2,32,128]{3,1,0,2:T(2,128)(2,1)S(1)} %copy.8), channel_id=1, source_target_pairs={{8,0},{12,4},{16,8},{20,12},{24,16},{28,20},{9,1},{13,5},{17,9},{2... | collective-permute-start | bytes 1572872 | tf_op jit(solution)/shard_map/ppermute | solution.py:24
  29.9 1.3 %collective-permute-start = (bf16[32,2,32,128]{3,1,0,2:T(2,128)(2,1)S(1)}, bf16[32,2,32,128]{3,1,0,2:T(2,128)(2,1)S(1)}, u32[]{:S(2)}, u32[]{:S(2)}) collective-permute-start(bf16[32,2,32,128]{3,1,0,2:T(2,128)(2,1)S(1)} %copy.8), channel_id=1, source_target_pairs={{4,0},{8,4},{12,8},{16,12},{20,16},{24,20},{28,24},{5,1},{9,5},{13... | collective-permute-start | bytes 1572872 | tf_op jit(solution)/shard_map/ppermute | solution.py:24
  31.2 1.5 %collective-permute-start.3 = (bf16[32,2,32,128]{3,1,0,2:T(2,128)(2,1)S(1)}, bf16[32,2,32,128]{3,1,0,2:T(2,128)(2,1)S(1)}, u32[]{:S(2)}, u32[]{:S(2)}) collective-permute-start(bf16[32,2,32,128]{3,1,0,2:T(2,128)(2,1)S(1)} %copy.8), channel_id=1, source_target_pairs={{16,0},{20,4},{24,8},{28,12},{17,1},{21,5},{25,9},{29,13},{18,2},{... | collective-permute-start | bytes 1572872 | tf_op jit(solution)/shard_map/ppermute | solution.py:24
  32.7 0.9 fusion.32
  33.7 0.5 copy_dynamic-update-slice_fusion
  34.2 1.2 %pad_maximum_fusion.3 = bf16[32,2,32,128]{3,1,0,2:T(2,128)(2,1)S(1)} fusion(bf16[32,1,32,128]{3,1,0,2:T(2,128)(2,1)S(1)} %get-tuple-element.9, bf16[32,1,32,128]{3,1,0,2:T(2,128)(2,1)S(1)} %get-tuple-element.8), kind=kLoop, calls=%fused_computation.36 | loop fusion | flops 1048576 | bytes 1048576 | tf_op jit(solution)/shard_map/stack | solution.py:71
  35.4 0.5 copy.7
  36.0 19.4 %collective-permute-done = bf16[32,2,32,128]{3,1,0,2:T(2,128)(2,1)S(1)} collective-permute-done((bf16[32,2,32,128]{3,1,0,2:T(2,128)(2,1)S(1)}, bf16[32,2,32,128]{3,1,0,2:T(2,128)(2,1)S(1)}, u32[]{:S(2)}, u32[]{:S(2)}) %collective-permute-start) | collective-permute-done | bytes 524320 | tf_op jit(solution)/shard_map/ppermute | solution.py:24
  55.3 0.5 bitcast_dynamic-update-slice_fusion.3
  55.9 0.5 bitcast_dynamic-update-slice_fusion.2
  56.4 0.5 bitcast_dynamic-update-slice_fusion.1
  56.9 44.6 %collective-permute-done.3 = bf16[32,2,32,128]{3,1,0,2:T(2,128)(2,1)S(1)} collective-permute-done((bf16[32,2,32,128]{3,1,0,2:T(2,128)(2,1)S(1)}, bf16[32,2,32,128]{3,1,0,2:T(2,128)(2,1)S(1)}, u32[]{:S(2)}, u32[]{:S(2)}) %collective-permute-start.3) | collective-permute-done | bytes 524320 | tf_op jit(solution)/shard_map/ppermute | solution.py:24
  101.4 0.5 bitcast_dynamic-update-slice_fusion
  101.9 1.5 %constant_dynamic-slice_fusion.2 = (bf16[1,32,2,32,128]{4,2,1,3,0:T(2,128)(2,1)S(1)}, bf16[1,32,2,32,128]{4,2,1,3,0:T(2,128)(2,1)S(1)}, bf16[1,32,2,32,128]{4,2,1,3,0:T(2,128)(2,1)S(1)}) fusion(bf16[5,32,2,32,128]{4,2,1,3,0:T(2,128)(2,1)S(1)} %bitcast_dynamic-update-slice_fusion, s32[]{:T(128)S(6)} %select_n.41, s32[]{:T(128)S(6)} %select_n.47, s32[]{:T(128)S(6)} %select_n.44), kind=kLoop, calls=%fused_computation.59 | loop fusion | bytes 3145740 | tf_op jit(solution)/shard_map/jit(dynamic_index_in_dim)/dynamic_slice | solution.py:81
  103.4 0.9 fusion.4
  104.3 0.9 fusion.2
  105.3 0.9 fusion.3
  106.2 3.2 %pad_maximum_fusion = bf16[3,32,2,128,128]{4,3,2,1,0:T(8,128)(2,1)} fusion(bf16[1,32,2,128,128]{4,3,2,1,0:T(8,128)(2,1)S(1)} %fusion.4, bf16[1,32,2,128,128]{4,3,2,1,0:T(8,128)(2,1)S(1)} %fusion.3, bf16[1,32,2,128,128]{4,3,2,1,0:T(8,128)(2,1)S(1)} %fusion.2), kind=kLoop, calls=%fused_computation | loop fusion | flops 6291456 | bytes 12582912 | tf_op jit(solution)/shard_map/stack | solution.py:86
  (6 shorter events, 0.0 us)
Async XLA Ops:
  12.6 5.3 %copy-start = (s32[3]{0:T(128)S(1)}, s32[3]{0:T(128)}, u32[]{:S(2)}) copy-start(s32[3]{0:T(128)} %param.4) | copy-start | bytes 40
  13.7 13.1 %all-to-all-start = ((bf16[4,8,2,32,128]{4,3,2,1,0:T(8,128)(2,1)}), bf16[4,8,2,32,128]{4,3,2,1,0:T(8,128)(2,1)S(1)}, u32[]{:S(2)}, u32[]{:S(2)}) async-start(bf16[4,8,2,32,128]{4,3,2,1,0:T(8,128)(2,1)} %pad_maximum_fusion.2), calls=%async_computation | async-start | bytes 1048576 | tf_op jit(solution)/shard_map/all_to_all | solution.py:17
  27.3 29.0 %collective-permute-start.2 = (bf16[32,2,32,128]{3,1,0,2:T(2,128)(2,1)S(1)}, bf16[32,2,32,128]{3,1,0,2:T(2,128)(2,1)S(1)}, u32[]{:S(2)}, u32[]{:S(2)}) collective-permute-start(bf16[32,2,32,128]{3,1,0,2:T(2,128)(2,1)S(1)} %copy.8), channel_id=1, source_target_pairs={{12,0},{16,4},{20,8},{24,12},{28,16},{13,1},{17,5},{21,9},{25,13},... | collective-permute-start | bytes 1572872 | tf_op jit(solution)/shard_map/ppermute | solution.py:24
  28.6 27.2 %collective-permute-start.1 = (bf16[32,2,32,128]{3,1,0,2:T(2,128)(2,1)S(1)}, bf16[32,2,32,128]{3,1,0,2:T(2,128)(2,1)S(1)}, u32[]{:S(2)}, u32[]{:S(2)}) collective-permute-start(bf16[32,2,32,128]{3,1,0,2:T(2,128)(2,1)S(1)} %copy.8), channel_id=1, source_target_pairs={{8,0},{12,4},{16,8},{20,12},{24,16},{28,20},{9,1},{13,5},{17,9},{2... | collective-permute-start | bytes 1572872 | tf_op jit(solution)/shard_map/ppermute | solution.py:24
  29.9 25.4 %collective-permute-start = (bf16[32,2,32,128]{3,1,0,2:T(2,128)(2,1)S(1)}, bf16[32,2,32,128]{3,1,0,2:T(2,128)(2,1)S(1)}, u32[]{:S(2)}, u32[]{:S(2)}) collective-permute-start(bf16[32,2,32,128]{3,1,0,2:T(2,128)(2,1)S(1)} %copy.8), channel_id=1, source_target_pairs={{4,0},{8,4},{12,8},{16,12},{20,16},{24,20},{28,24},{5,1},{9,5},{13... | collective-permute-start | bytes 1572872 | tf_op jit(solution)/shard_map/ppermute | solution.py:24
  31.2 70.2 %collective-permute-start.3 = (bf16[32,2,32,128]{3,1,0,2:T(2,128)(2,1)S(1)}, bf16[32,2,32,128]{3,1,0,2:T(2,128)(2,1)S(1)}, u32[]{:S(2)}, u32[]{:S(2)}) collective-permute-start(bf16[32,2,32,128]{3,1,0,2:T(2,128)(2,1)S(1)} %copy.8), channel_id=1, source_target_pairs={{16,0},{20,4},{24,8},{28,12},{17,1},{21,5},{25,9},{29,13},{18,2},{... | collective-permute-start | bytes 1572872 | tf_op jit(solution)/shard_map/ppermute | solution.py:24
